TPU v7x, 256 devices: a whole 4x4x8 slice. The times are simulated.
256 devices in a mesh: col: 64 (over y, z_lo, x, core), row: 4 (over z_hi).
Axes of the slice: x: 4, y: 4, z: 8 (z_hi: 4, z_lo: 2; z = z_hi * 2 + z_lo), core: 2. Of those that a mesh axis runs over, the one named last changes fastest.
Arguments:
- root_inverse: float32 [2048, 2048], P('row', 'col')
- child_inverse: float32 [256, 512, 512], P(('col', 'row'))
- child_panel: float32 [256, 1024, 512], P(('col', 'row')), may hold values from -0.375 to 0.375
- structure: int32 [256, 8], P(('col', 'row')), may hold values from 0 to 15, as said below
- widths: int32 [256], P(('col', 'row')), may hold values from 256 to 512
Outputs:
- sigma_root: float32 [2048, 2048], P('row', 'col')
- child_cross: float32 [256, 1024, 512], P(('col', 'row'))
- child_variance: float32 [256, 512], P(('col', 'row'))
Inputs may be any that keep to these rules, and one draw needn't show every extreme that they name: `structure`: each child names 8 distinct root blocks in rising order.
All inputs are finite; a program needn't handle non-finite values.
Results may differ from a plain program's by a relative error of at most 0.0003.
Values sent between devices are 32-bit elements; how exact they have to be, the bound alone decides.
No kernel may reach another device: no remote copies, remote signals or barrier semaphores. Data moves between devices by JAX's collectives and lax.ppermute only.
A program may use at most 192 MiB of HBM per device.

v0:
```python
import jax
import jax.numpy as jnp
from jax import lax
from jax.sharding import PartitionSpec as P

TILE = 128


def body(root_inverse, child_inverse, child_panel, structure, widths):
    partial_value = jnp.dot(
        lax.all_gather(root_inverse, "col", axis=1, tiled=True).T,
        root_inverse,
        precision=lax.Precision.HIGHEST,
        preferred_element_type=jnp.float32,
    )
    own_block = lax.psum_scatter(partial_value, "row", scatter_dimension=0, tiled=True)
    wide_rows = lax.all_gather(own_block, "col", axis=1, tiled=True)
    complete = lax.all_gather(wide_rows, "row", axis=0, tiled=True)
    tile_count = complete.shape[0] // TILE
    tiled = complete.reshape(tile_count, TILE, tile_count, TILE)

    def handle(items):
        inverse_block, panel_block, tiles, width_value = items
        column_ids = jnp.arange(inverse_block.shape[0], dtype=jnp.int32)
        live_cols = (column_ids < width_value).astype(jnp.float32)
        masked_inverse = inverse_block * live_cols[:, None] * live_cols[None, :]
        masked_panel = panel_block * live_cols[None, :]
        update = jnp.dot(
            masked_panel,
            masked_inverse,
            precision=lax.Precision.HIGHEST,
            preferred_element_type=jnp.float32,
        )
        picked = jnp.take(jnp.take(tiled, tiles, axis=0), tiles, axis=2)
        ancestor_block = picked.reshape(tiles.shape[0] * TILE, tiles.shape[0] * TILE)
        cross_block = -jnp.dot(
            ancestor_block,
            update,
            precision=lax.Precision.HIGHEST,
            preferred_element_type=jnp.float32,
        )
        variance = jnp.sum(masked_inverse * masked_inverse, axis=0) - jnp.sum(
            update * cross_block, axis=0
        )
        return (cross_block, variance)

    child_cross, child_variance = lax.map(handle, (child_inverse, child_panel, structure, widths))
    return (own_block, child_cross, child_variance)


def solution(mesh):
    placed = (
        P("row", "col"),
        P(("col", "row"), None, None),
        P(("col", "row"), None, None),
        P(("col", "row"), None),
        P(("col", "row")),
    )
    return jax.shard_map(
        body,
        mesh=mesh,
        in_specs=placed,
        out_specs=(P("row", "col"), P(("col", "row"), None, None), P(("col", "row"), None)),
        check_vma=False,
    )
```

profile of v0, /device:TPU:1, one launch (start us, length us, event | category | flops | bytes accessed | tf_op | source)
XLA Modules:
  0.0 641.0 jit_solution(5670676339828152946)
XLA Ops:
  7.2 0.0 all-gather.4.cloned.1.call-start
  7.2 0.7 all-gather.4.cloned.1.call-update
  7.9 0.0 copy-start.1
  7.9 0.0 copy-start
  7.9 0.0 reduce-scatter.2.cloned.1.call-start
  8.0 114.6 %all-gather.4.cloned.1.call-done = f32[512,2048]{0,1:T(8,128)} async-done(((f32[512,32]{0,1:T(8,128)}), f32[512,2048]{0,1:T(8,128)}) %all-gather.4.cloned.1.call-update) | async-done | bytes 4194320 | tf_op jit(solution)/shard_map/all_gather | solution.py:11
  122.5 6.8 %fusion.19 = f32[2048,32]{0,1:T(8,128)} fusion(f32[512,2048]{0,1:T(8,128)} %all-gather.4.cloned.1.call-done, f32[512,32]{0,1:T(8,128)} %param.5), kind=kOutput, calls=%fused_computation.32 | convolution fusion | flops 402653184 | bytes 4521984 | tf_op jit(solution)/shard_map/dot_general | solution.py:10
  129.3 0.0 reduce-scatter.2.cloned.1.call-update
  129.3 0.0 all-gather.6.cloned.1.call-start
  129.4 21.8 %reduce-scatter.2.cloned.1.call-done = f32[512,32]{0,1:T(8,128)} async-done(((f32[2048,32]{0,1:T(8,128)}), f32[512,32]{0,1:T(8,128)}) %reduce-scatter.2.cloned.1.call-update) | async-done | bytes 65552 | tf_op jit(solution)/shard_map/reduce_scatter | solution.py:16
  151.2 0.0 all-gather.6.cloned.1.call-update
  151.2 0.0 all-gather.8.cloned.1.call-start
  151.3 112.2 %all-gather.6.cloned.1.call-done = f32[512,2048]{0,1:T(8,128)} async-done(((f32[512,32]{0,1:T(8,128)}), f32[512,2048]{0,1:T(8,128)}) %all-gather.6.cloned.1.call-update) | async-done | bytes 4194320 | tf_op jit(solution)/shard_map/all_gather | solution.py:17
  263.5 0.0 all-gather.8.cloned.1.call-update
  264.2 0.0 copy-done.1
  264.2 0.0 copy-done
  264.2 0.2 fusion.9
  264.4 0.1 broadcast_bitcast_fusion
  264.5 5.2 fusion.2
  269.7 289.6 %all-gather.8.cloned.1.call-done = f32[2048,2048]{0,1:T(8,128)} async-done(((f32[512,2048]{0,1:T(8,128)}), f32[2048,2048]{0,1:T(8,128)}) %all-gather.8.cloned.1.call-update) | async-done | bytes 16777232 | tf_op jit(solution)/shard_map/all_gather | solution.py:18
  559.3 14.1 %copy.14 = f32[256,8,16,128]{3,2,1,0:T(8,128)} copy(f32[256,8,16,128]{3,1,2,0:T(8,128)} %bitcast.45) | data formatting | bytes 33554432
  573.4 21.5 %copy.11 = f32[16,128,16,128]{3,2,1,0:T(8,128)} copy(f32[16,128,16,128]{1,0,3,2:T(8,128)} %bitcast.43) | data formatting | bytes 33554432 | tf_op jit(solution)/shard_map/reshape | solution.py:20
  594.8 10.1 %gather_fusion = f32[8,128,16,128]{3,2,1,0:T(8,128)} fusion(f32[16,128,16,128]{3,2,1,0:T(8,128)} %copy.11, s32[1024]{0:T(1024)S(1)} %pad_clamp_fusion), kind=kCustom, calls=%fused_computation | custom fusion | bytes 16777248 | tf_op jit(solution)/shard_map/while/body/eval_jaxpr/jit(_take)/gather | solution.py:34
  604.9 4.2 broadcast_select_fusion
  609.1 5.7 copy.12
  614.8 6.2 gather_fusion.1
  621.0 4.6 copy.13
  625.5 8.3 %multiply_reduce_fusion = (f32[512]{0:T(512)S(1)}, f32[1,1024,512]{2,1,0:T(8,128)}) fusion(f32[1024,512]{1,0:T(8,128)S(1)} %fusion.2, f32[128,8,8,128]{3,2,1,0:T(8,128)S(1)} %bitcast.44, pred[1024]{0:T(1024)(128)(4,1)S(1)} %broadcast_bitcast_fusion), kind=kOutput, calls=%fused_computation.8 | convolution fusion | flops 6445071872 | bytes 8391680 | tf_op jit(solution)/shard_map/while/body/eval_jaxpr/dot_general | solution.py:36
  633.9 0.6 sub.14
  (4 shorter events, 0.0 us)
Async XLA Ops:
  7.2 115.4 %all-gather.4.cloned.1.call-start = ((), (), s32[]{:S(2)}) async-start(), calls=%async_computation.1 | async-start | bytes 4259840 | tf_op jit(solution)/shard_map/all_gather | solution.py:11
  7.9 256.3 %copy-start.1 = (s32[1,8]{1,0:T(1,128)S(1)}, s32[1,8]{1,0:T(1,128)}, u32[]{:S(2)}) copy-start(s32[1,8]{1,0:T(1,128)} %param.8) | copy-start | bytes 100
  7.9 256.3 %copy-start = (f32[1,512,512]{2,1,0:T(8,128)S(1)}, f32[1,512,512]{2,1,0:T(8,128)}, u32[]{:S(2)}) copy-start(f32[1,512,512]{2,1,0:T(8,128)} %param.6) | copy-start | bytes 3145732
  7.9 143.3 %reduce-scatter.2.cloned.1.call-start = ((), (), s32[]{:S(2)}) async-start(), calls=%async_computation.2 | async-start | bytes 327680 | tf_op jit(solution)/shard_map/reduce_scatter | solution.py:16
  129.3 134.1 %all-gather.6.cloned.1.call-start = ((), (), s32[]{:S(2)}) async-start(), calls=%async_computation.3 | async-start | bytes 4259840 | tf_op jit(solution)/shard_map/all_gather | solution.py:17
  151.2 408.0 %all-gather.8.cloned.1.call-start = ((), (), s32[]{:S(2)}) async-start(), calls=%async_computation.4 | async-start | bytes 20971520 | tf_op jit(solution)/shard_map/all_gather | solution.py:18
Sparse Core Ops, SparseCore 0:
  9.9 112.6 all-gather.3
  129.5 21.7 reduce-scatter.1
  153.8 109.6 all-gather.5
  265.3 293.9 all-gather.7
where the time goes:
time: 641 us
  waiting for transfers between devices  539 us (84%)
  local copies, waits for them, and re-layouts  62.2 us (10%)
  matrix products  20.3 us (3%)
  between operations  14.5 us (2%)
    all_gather x1, waiting for transfers between devices, body(): complete = lax.all_gather(wide_rows, 'row', axis=0, tiled=True)  290 us
    all_gather x1, waiting for transfers between devices, body(): lax.all_gather(root_inverse, 'col', axis=1, tiled=True)  115 us
    all_gather x1, waiting for transfers between devices, body(): wide_rows = lax.all_gather(own_block, 'col', axis=1, tiled=True)  112 us
    reduce_scatter x1, waiting for transfers between devices, body(): lax.psum_scatter(partial_value, 'row', scatter_dimension=0, tiled=True)  21.8 us
    reshape x1, local copies, waits for them, and re-layouts, body(): tiled = complete.reshape(tile_count, TILE, tile_count, TILE)  21.5 us
    gather x3, local copies, waits for them, and re-layouts, handle(): picked = jnp.take(jnp.take(tiled, tiles, axis=0), tiles, axis=2)  20.8 us
    unnamed x5, local copies, waits for them, and re-layouts  14.1 us
  transfers between devices with their start and end apart: 4, of which 4 were waited for; matrix products, arithmetic and copies ran while one was open for 1% of the time, Pallas kernels for 0%

commit v1 on v0

--- a/solution.py
+++ b/solution.py
@@ -15,7 +15,15 @@
     )
     own_block = lax.psum_scatter(partial_value, "row", scatter_dimension=0, tiled=True)
     wide_rows = lax.all_gather(own_block, "col", axis=1, tiled=True)
-    complete = lax.all_gather(wide_rows, "row", axis=0, tiled=True)
+    complete = jnp.concatenate(
+        lax.all_to_all(
+            jnp.stack([wide_rows for _ in range(lax.axis_size("row"))], axis=0),
+            axis_name="row",
+            split_axis=0,
+            concat_axis=0,
+        ),
+        0,
+    )
     tile_count = complete.shape[0] // TILE
     tiled = complete.reshape(tile_count, TILE, tile_count, TILE)
 

time: 641 us -> 714 us (1.11)
  waiting for transfers between devices: 539 us -> 610 us
    all_to_all x0 -> x1, waiting for transfers between devices: none -> 361 us  [body(): lax.all_to_all(jnp.stack([wide_rows for _ in range(lax.axis_size('row'))]...]
    all_gather x1 -> x0, waiting for transfers between devices: 290 us -> none  [body(): complete = lax.all_gather(wide_rows, 'row', axis=0, tiled=True)]
    reshape x1 -> x0, local copies, waits for them, and re-layouts: 21.5 us -> none  [body(): tiled = complete.reshape(tile_count, TILE, tile_count, TILE)]
    another operation x0 -> x1, local copies, waits for them, and re-layouts: none -> 10.1 us  [body(): jnp.stack([wide_rows for _ in range(lax.axis_size('row'))], axis=0)]
where the time goes in v1:
time: 714 us; the launch traced here: 713 us
  waiting for transfers between devices  610 us (85%)
  local copies, waits for them, and re-layouts  56.2 us (8%)
  matrix products  20.3 us (3%)
  between operations  14.5 us (2%)
  starting transfers between devices  7.21 us (1%)
    all_to_all x1, waiting for transfers between devices, body(): lax.all_to_all(jnp.stack([wide_rows for _ in range(lax.axis_size('row'))]...  361 us
    all_gather x1, waiting for transfers between devices, body(): lax.all_gather(root_inverse, 'col', axis=1, tiled=True)  115 us
    all_gather x1, waiting for transfers between devices, body(): wide_rows = lax.all_gather(own_block, 'col', axis=1, tiled=True)  112 us
    reduce_scatter x1, waiting for transfers between devices, body(): lax.psum_scatter(partial_value, 'row', scatter_dimension=0, tiled=True)  21.9 us
    gather x3, local copies, waits for them, and re-layouts, handle(): picked = jnp.take(jnp.take(tiled, tiles, axis=0), tiles, axis=2)  20.8 us
  transfers between devices with their start and end apart: 4, of which 4 were waited for; matrix products, arithmetic and copies ran while one was open for 1% of the time, Pallas kernels for 0%

profile of v1, /device:TPU:1, one launch (start us, length us, event | category | flops | bytes accessed | tf_op | source)
XLA Modules:
  0.0 713.3 jit_solution(10571682048371239800)
XLA Ops:
  7.2 0.0 all-gather.3.cloned.1.call-start
  7.2 0.7 all-gather.3.cloned.1.call-update
  7.9 0.0 reduce-scatter.2.cloned.1.call-start
  7.9 114.6 %all-gather.3.cloned.1.call-done = f32[512,2048]{0,1:T(8,128)} async-done(((f32[512,32]{0,1:T(8,128)}), f32[512,2048]{0,1:T(8,128)}) %all-gather.3.cloned.1.call-update) | async-done | bytes 4194320 | tf_op jit(solution)/shard_map/all_gather | solution.py:11
  122.5 6.8 fusion.19
  129.3 0.0 reduce-scatter.2.cloned.1.call-update
  129.3 0.0 all-gather.5.cloned.1.call-start
  129.4 21.9 %reduce-scatter.2.cloned.1.call-done = f32[512,32]{0,1:T(8,128)} async-done(((f32[2048,32]{0,1:T(8,128)}), f32[512,32]{0,1:T(8,128)}) %reduce-scatter.2.cloned.1.call-update) | async-done | bytes 65552 | tf_op jit(solution)/shard_map/reduce_scatter | solution.py:16
  151.2 0.0 all-gather.5.cloned.1.call-update
  151.3 112.2 %all-gather.5.cloned.1.call-done = f32[512,2048]{0,1:T(8,128)} async-done(((f32[512,32]{0,1:T(8,128)}), f32[512,2048]{0,1:T(8,128)}) %all-gather.5.cloned.1.call-update) | async-done | bytes 4194320 | tf_op jit(solution)/shard_map/all_gather | solution.py:17
  263.5 5.5 copy.10
  269.0 10.1 %stack.2 = f32[4,512,2048]{2,1,0:T(8,128)} broadcast(f32[512,2048]{1,0:T(8,128)} %copy.10), dimensions={1,2} | broadcast | bytes 20971520 | tf_op jit(solution)/shard_map/stack | solution.py:20
  279.0 0.0 copy-start.1
  279.0 0.0 copy-start
  279.0 7.1 all-to-all-start
  286.8 0.0 copy-done.1
  286.8 0.0 copy-done
  286.8 0.2 fusion.9
  287.1 0.1 broadcast_bitcast_fusion
  287.1 5.2 fusion.2
  292.3 360.7 %all-to-all-done = f32[4,512,2048]{2,1,0:T(8,128)} async-done(((f32[4,512,2048]{2,1,0:T(8,128)}), f32[4,512,2048]{2,1,0:T(8,128)}, u32[]{:S(2)}, u32[]{:S(2)}) %all-to-all-start) | async-done | bytes 16777248 | tf_op jit(solution)/shard_map/all_to_all | solution.py:19
  653.1 14.1 %copy.13 = f32[256,8,16,128]{3,2,1,0:T(8,128)} copy(f32[256,8,16,128]{3,1,2,0:T(8,128)} %bitcast.12) | data formatting | bytes 33554432
  667.1 10.1 %gather_fusion = f32[8,128,16,128]{3,2,1,0:T(8,128)} fusion(f32[16,128,16,128]{3,2,1,0:T(8,128)} %bitcast.42, s32[1024]{0:T(1024)S(1)} %pad_clamp_fusion), kind=kCustom, calls=%fused_computation | custom fusion | bytes 16777248 | tf_op jit(solution)/shard_map/while/body/eval_jaxpr/jit(_take)/gather | solution.py:42
  677.2 4.2 broadcast_select_fusion
  681.4 5.7 copy.11
  687.1 6.1 gather_fusion.1
  693.3 4.6 copy.12
  697.8 8.3 %multiply_reduce_fusion = (f32[512]{0:T(512)S(1)}, f32[1,1024,512]{2,1,0:T(8,128)}) fusion(f32[1024,512]{1,0:T(8,128)S(1)} %fusion.2, f32[128,8,8,128]{3,2,1,0:T(8,128)S(1)} %bitcast.43, pred[1024]{0:T(1024)(128)(4,1)S(1)} %broadcast_bitcast_fusion), kind=kOutput, calls=%fused_computation.8 | convolution fusion | flops 6445071872 | bytes 8391680 | tf_op jit(solution)/shard_map/while/body/eval_jaxpr/dot_general | solution.py:44
  706.2 0.6 sub.14
  (4 shorter events, 0.0 us)
Async XLA Ops:
  7.2 115.4 %all-gather.3.cloned.1.call-start = ((), (), s32[]{:S(2)}) async-start(), calls=%async_computation.2 | async-start | bytes 4259840 | tf_op jit(solution)/shard_map/all_gather | solution.py:11
  7.9 143.3 %reduce-scatter.2.cloned.1.call-start = ((), (), s32[]{:S(2)}) async-start(), calls=%async_computation.3 | async-start | bytes 327680 | tf_op jit(solution)/shard_map/reduce_scatter | solution.py:16
  129.3 134.1 %all-gather.5.cloned.1.call-start = ((), (), s32[]{:S(2)}) async-start(), calls=%async_computation.4 | async-start | bytes 4259840 | tf_op jit(solution)/shard_map/all_gather | solution.py:17
  279.0 7.8 %copy-start.1 = (s32[1,8]{1,0:T(1,128)S(1)}, s32[1,8]{1,0:T(1,128)}, u32[]{:S(2)}) copy-start(s32[1,8]{1,0:T(1,128)} %param.8) | copy-start | bytes 100
  279.0 7.8 %copy-start = (f32[1,512,512]{2,1,0:T(8,128)S(1)}, f32[1,512,512]{2,1,0:T(8,128)}, u32[]{:S(2)}) copy-start(f32[1,512,512]{2,1,0:T(8,128)} %param.6) | copy-start | bytes 3145732
  279.0 374.0 %all-to-all-start = ((f32[4,512,2048]{2,1,0:T(8,128)}), f32[4,512,2048]{2,1,0:T(8,128)}, u32[]{:S(2)}, u32[]{:S(2)}) async-start(f32[4,512,2048]{2,1,0:T(8,128)} %stack.2), calls=%async_computation.1 | async-start | bytes 33554432 | tf_op jit(solution)/shard_map/all_to_all | solution.py:19
Sparse Core Ops, SparseCore 0:
  9.9 112.6 all-gather.2
  129.5 21.7 reduce-scatter.1
  153.8 109.6 all-gather.4
